TPU v7x, 32 devices: a whole 2x2x4 slice. The times are simulated.
32 devices in a mesh: grp: 4 (over y, x), seq: 4 (over z), mlp: 2 (over core).
Axes of the slice: x: 2, y: 2, z: 4, core: 2. Of those that a mesh axis runs over, the one named last changes fastest.
Arguments:
- queries: bfloat16 [16, 4, 4096], P('grp'), may hold values from -6 to 6
- new_keys: bfloat16 [16, 4, 4096], P(('grp', 'seq')), may hold values from -6 to 6
- new_values: bfloat16 [16, 4, 4096], P(('grp', 'seq')), may hold values from -6 to 6
- prefix_keys: bfloat16 [4, 2048, 4096], P('grp', ('seq', 'mlp')), may hold values from -250 to 250
- prefix_values: bfloat16 [4, 2048, 4096], P('grp', ('seq', 'mlp')), may hold values from -6 to 6
- tail_keys: bfloat16 [16, 256, 4096], P(('grp', 'seq'), 'mlp'), may hold values from -6 to 6
- tail_values: bfloat16 [16, 256, 4096], P(('grp', 'seq'), 'mlp'), may hold values from -6 to 6
- prefix_len: int32 [4], P('grp'), may hold values from 1 to 2048, as said below
- tail_len: int32 [16], P('grp'), may hold values from 0 to 256, as said below
- resid: bfloat16 [16, 4, 4096], P('grp', None, ('seq', 'mlp')), may hold values from -12 to 12
- w_out: bfloat16 [4096, 4096], P(None, ('seq', 'mlp')), may hold values from -0.09375 to 0.09375
- ln_gain: bfloat16 [4096], P(('seq', 'mlp')), may hold values from 0.25 to 1.75
- w_up: bfloat16 [4096, 16384], P(('seq', 'mlp'), 'grp'), may hold values from -0.09375 to 0.09375
- w_down: bfloat16 [16384, 4096], P('grp', ('seq', 'mlp')), may hold values from -0.046875 to 0.046875
Outputs:
- out: float32 [16, 4, 4096], P('grp', None, ('seq', 'mlp'))
Inputs may be any that keep to these rules, and one draw needn't show every extreme that they name: `prefix_len`: every group's live prefix is 1 to 2048 slots; in every draw some group's prefix fills all 2048 slots. `tail_len`: A request's live tail is 0 to 256 slots; in every draw some request's tail fills all 256 slots.
All inputs are finite; a program needn't handle non-finite values.
Results may differ from a plain program's by a relative error of at most 0.0075.
Values may be sent and summed in bfloat16 or wider, within the bound.
A program may use at most 128 MiB of HBM per device.

v0:
```python
import math
import jax
import jax.numpy as jnp
from jax import lax
from jax.sharding import PartitionSpec as P

D = 4096
H = 32
NEG = -1e30


def merged(value, axis, join):
    pieces = jax.tree.map(lambda part: lax.all_gather(part, axis), value)
    head = jax.tree.map(lambda part: part[0], pieces)
    tail = jax.tree.map(lambda part: part[1:], pieces)
    so_far, _ = lax.scan(lambda so_far, piece: (join(so_far, piece), None), head, tail)
    return so_far


def head_slopes(count):
    return jnp.power(2.0, -8.0 * (jnp.arange(count, dtype=jnp.float32) + 1.0) / count)


def attend(query_rows, key_block, value_block, query_pos, key_pos, key_mask):
    head_count = query_rows.shape[1]
    inv_scale = 1.0 / math.sqrt(query_rows.shape[2])
    scores = (
        jnp.einsum("qhd,khd->hqk", query_rows, key_block, preferred_element_type=jnp.float32)
        * inv_scale
    )
    distance = (query_pos[:, None] - key_pos[None, :]).astype(jnp.float32)
    scores = scores - head_slopes(head_count)[:, None, None] * distance[None, :, :]
    scores = jnp.where(key_mask, scores, NEG)
    row_max = jnp.max(scores, axis=2)
    weights = jnp.where(key_mask, jnp.exp(scores - row_max[:, :, None]), 0.0)
    weight_sum = jnp.sum(weights, axis=2)
    mixed_sum = jnp.einsum(
        "hqk,khd->qhd",
        weights.astype(jnp.bfloat16),
        value_block,
        preferred_element_type=jnp.float32,
    )
    return (row_max.T, weight_sum.T, mixed_sum)


def join_parts(first, second):
    best_max = jnp.maximum(first[0], second[0])
    factor_one = jnp.exp(first[0] - best_max)
    factor_two = jnp.exp(second[0] - best_max)
    return (
        best_max,
        first[1] * factor_one + second[1] * factor_two,
        first[2] * factor_one[:, :, None] + second[2] * factor_two[:, :, None],
    )


def body(
    queries,
    new_keys,
    new_values,
    prefix_keys,
    prefix_values,
    tail_keys,
    tail_values,
    prefix_len,
    tail_len,
    resid,
    w_out,
    ln_gain,
    w_up,
    w_down,
):
    group_req, step_count, model_width = queries.shape
    head_dim = model_width // H
    row_count = group_req * step_count
    seq_index = lax.axis_index("seq")
    core_index = lax.axis_index("mlp")
    block_len = prefix_keys.shape[1]
    tail_block = tail_keys.shape[1]
    block_start = (seq_index * lax.axis_size("mlp") + core_index) * block_len
    prefix_end = prefix_len[0]
    step_index = jnp.arange(step_count, dtype=jnp.int32)
    query_pos = prefix_end + jnp.repeat(tail_len, step_count) + jnp.tile(step_index, group_req)
    query_rows = queries.reshape(row_count, H, head_dim)
    key_pos = block_start + jnp.arange(block_len, dtype=jnp.int32)
    key_live = key_pos < prefix_end
    own_len = lax.dynamic_index_in_dim(tail_len, seq_index, 0, keepdims=False)
    own_rows = lax.dynamic_slice_in_dim(query_rows, seq_index * step_count, step_count, 0)
    own_pos = prefix_end + own_len + step_index
    tail_index = core_index * tail_block + jnp.arange(tail_block, dtype=jnp.int32)
    partial_value = attend(
        query_rows,
        prefix_keys[0].reshape(block_len, H, head_dim),
        prefix_values[0].reshape(block_len, H, head_dim),
        query_pos,
        key_pos,
        key_live[None, None, :],
    )
    tail_result = attend(
        own_rows,
        tail_keys[0].reshape(tail_block, H, head_dim),
        tail_values[0].reshape(tail_block, H, head_dim),
        own_pos,
        prefix_end + tail_index,
        (tail_index < own_len)[None, None, :],
    )
    self_mask = (step_index[None, :] <= step_index[:, None]) & (core_index == 0)
    self_result = attend(
        own_rows,
        new_keys[0].reshape(step_count, H, head_dim),
        new_values[0].reshape(step_count, H, head_dim),
        own_pos,
        own_pos,
        self_mask[None, :, :],
    )
    own_slice = tuple(
        (
            lax.dynamic_slice_in_dim(member, seq_index * step_count, step_count, 0)
            for member in partial_value
        )
    )
    own_part = join_parts(join_parts(own_slice, tail_result), self_result)
    partial_value = tuple(
        (
            lax.dynamic_update_slice_in_dim(member, update, seq_index * step_count, 0)
            for member, update in zip(partial_value, own_part)
        )
    )
    row_max, weight_sum, mixed_sum = merged(
        (partial_value[0], partial_value[1], partial_value[2]), ("seq", "mlp"), join_parts
    )
    attention = (
        (mixed_sum / weight_sum[:, :, None]).astype(jnp.bfloat16).reshape(row_count, model_width)
    )
    width_block = resid.shape[2]
    stream = resid.astype(jnp.float32).reshape(row_count, width_block) + jnp.dot(
        attention, w_out, preferred_element_type=jnp.float32
    )
    row_sums, squares = lax.psum(
        (jnp.sum(stream, axis=1), jnp.sum(stream * stream, axis=1)), ("seq", "mlp")
    )
    row_mean = row_sums / D
    row_var = squares / D - row_mean * row_mean
    hidden = (
        (stream - row_mean[:, None])
        * lax.rsqrt(row_var[:, None] + 1e-05)
        * ln_gain.astype(jnp.float32)
    ).astype(jnp.bfloat16)
    lifted = jnp.dot(
        lax.all_gather(hidden, "grp", axis=0, tiled=True), w_up, preferred_element_type=jnp.float32
    )
    summed = lax.psum(lifted, ("seq", "mlp"))
    activated = jax.nn.gelu(summed, approximate=False).astype(jnp.bfloat16)
    projected = lax.psum_scatter(
        jnp.dot(activated, w_down, preferred_element_type=jnp.float32),
        "grp",
        scatter_dimension=0,
        tiled=True,
    )
    return (stream + projected).reshape(group_req, step_count, width_block)


def solution(mesh):
    return jax.shard_map(
        body,
        mesh=mesh,
        in_specs=(
            P("grp", None, None),
            P(("grp", "seq"), None, None),
            P(("grp", "seq"), None, None),
            P("grp", ("seq", "mlp"), None),
            P("grp", ("seq", "mlp"), None),
            P(("grp", "seq"), "mlp", None),
            P(("grp", "seq"), "mlp", None),
            P("grp"),
            P("grp"),
            P("grp", None, ("seq", "mlp")),
            P(None, ("seq", "mlp")),
            P(("seq", "mlp")),
            P(("seq", "mlp"), "grp"),
            P("grp", ("seq", "mlp")),
        ),
        out_specs=P("grp", None, ("seq", "mlp")),
        check_vma=False,
    )
```

profile of v0, /device:TPU:0, one launch (start us, length us, event | category | flops | bytes accessed | tf_op | source)
XLA Modules:
  0.0 181.5 jit_solution(5606925134826433128)
XLA Ops:
  7.4 1.2 dynamic_slice.28
  9.2 0.6 fusion.102
  9.9 1.1 reshape.182
  11.0 1.4 copy.98
  12.5 0.7 fusion.143
  14.4 1.2 fusion.142
  17.4 1.0 fusion.3
  19.1 0.5 fusion.22
  19.8 0.8 copy.92
  21.0 15.8 %all_gather.32 = f32[8,16,32]{2,1,0:T(8,128)S(1)} all-gather(f32[1,16,32]{2,1,0:T(8,128)S(1)} %copy.83), channel_id=1, replica_groups=mesh['grp'=4,'seq'=4,'mlp'=2] {'seq','mlp'}, dimensions={0}, use_global_device_ids=true | all-gather | bytes 18432 | tf_op jit(solution)/shard_map/all_gather | solution.py:13
  37.2 14.1 %all_gather.29 = f32[8,16,32]{2,1,0:T(8,128)S(1)} all-gather(f32[1,16,32]{2,1,0:T(8,128)S(1)} %copy.76), channel_id=1, replica_groups=mesh['grp'=4,'seq'=4,'mlp'=2] {'seq','mlp'}, dimensions={0}, use_global_device_ids=true | all-gather | bytes 18432 | tf_op jit(solution)/shard_map/all_gather | solution.py:13
  51.4 1.7 all-gather.2.cloned.1.call-done
  53.1 1.7 slice.29
  54.8 1.0 slice_bitcast_fusion
  55.8 2.2 %while.14 = (s32[]{:T(128)}, f32[16,32]{1,0:T(8,128)S(1)}, f32[16,32]{1,0:T(8,128)S(1)}, f32[16,32,128]{2,1,0:T(8,128)S(1)}, f32[7,16,32]{2,1,0:T(8,128)S(1)}, /...) while((s32[]{:T(128)}, f32[16,32]{1,0:T(8,128)S(1)}, f32[16,32]{1,0:T(8,128)S(1)}, ...), condition=%wide.region_7.8_spmd, body=%wide.region_6.7_spmd.sunk | while | flops 199682 | bytes 807005 | solution.py:16
  58.1 3.0 %fusion.137 = (f32[16]{0:T(128)S(1)}, f32[16]{0:T(128)S(1)}, f32[16,512]{1,0:T(8,128)S(1)}) fusion(f32[16,512]{1,0:T(8,128)S(1)} %reshape.186, bf16[4096,512]{1,0:T(8,128)(2,1)} %param.26, bf16[2,8,32,128]{3,2,1,0:T(8,128)(2,1)S(1)} %bitcast.177), kind=kOutput, calls=%fused_computation.181 | convolution fusion | flops 67141600 | bytes 4391040 | tf_op jit(solution)/shard_map/dot_general | solution.py:136
  61.1 15.5 %all-reduce = (f32[16]{0:T(128)S(1)}, f32[16]{0:T(128)S(1)}) all-reduce(f32[16]{0:T(128)S(1)} %get-tuple-element.60, f32[16]{0:T(128)S(1)} %get-tuple-element.59), channel_id=1, replica_groups=mesh['grp'=4,'seq'=4,'mlp'=2] {'seq','mlp'}, use_global_device_ids=true, to_apply=%region_11.12 | all-reduce | flops 32 | bytes 256 | tf_op jit(solution)/shard_map/psum | solution.py:139
  76.6 8.1 %all_gather.36 = bf16[64,512]{1,0:T(8,128)(2,1)S(1)} all-gather(bf16[16,512]{1,0:T(8,128)(2,1)S(1)} %multiply_convert_fusion), channel_id=1, replica_groups=mesh['grp'=4,'seq'=4,'mlp'=2] {'grp'}, dimensions={0}, use_global_device_ids=true | all-gather | bytes 81920 | tf_op jit(solution)/shard_map/all_gather | solution.py:150
  84.8 4.1 %fusion.144 = f32[64,4096]{1,0:T(8,128)} fusion(bf16[64,512]{1,0:T(8,128)(2,1)S(1)} %all_gather.36, bf16[512,4096]{1,0:T(8,128)(2,1)} %param.28), kind=kOutput, calls=%fused_computation.184 | convolution fusion | flops 268435456 | bytes 5308416 | tf_op jit(solution)/shard_map/dot_general | solution.py:149
  88.9 56.1 %all-reduce.3.cloned.1.call-done = f32[64,4096]{1,0:T(8,128)} async-done(((f32[64,4096]{1,0:T(8,128)}), f32[64,4096]{1,0:T(8,128)}) %all-reduce.3.cloned.1.call-update) | async-done | bytes 1048592 | tf_op jit(solution)/shard_map/psum | solution.py:152
  145.1 5.5 %fusion.37 = f32[64,512]{1,0:T(8,128)} fusion(bf16[4096,512]{1,0:T(8,128)(2,1)} %param.29, f32[64,4096]{1,0:T(8,128)} %all-reduce.3.cloned.1.call-done), kind=kOutput, calls=%fused_computation.49 | convolution fusion | flops 285474816 | bytes 5373952 | tf_op jit(solution)/shard_map/dot_general | solution.py:155
  150.6 22.9 %reduce-scatter.2.cloned.1.call-done = f32[16,512]{1,0:T(8,128)} async-done(((f32[64,512]{1,0:T(8,128)}), f32[16,512]{1,0:T(8,128)}) %reduce-scatter.2.cloned.1.call-update) | async-done | bytes 32784 | tf_op jit(solution)/shard_map/reduce_scatter | solution.py:154
  173.6 0.8 add.168
  174.3 0.6 reshape.184
  (85 shorter events, 6.9 us)
Async XLA Ops:
  6.5 13.1 %copy-start = (bf16[1,4,4096]{2,1,0:T(4,128)(2,1)S(1)}, bf16[1,4,4096]{2,1,0:T(4,128)(2,1)}, u32[]{:S(2)}) copy-start(bf16[1,4,4096]{2,1,0:T(4,128)(2,1)} %param.18) | copy-start | bytes 98308
  6.5 7.1 %copy-start.7 = (s32[4]{0:T(128)S(1)}, s32[4]{0:T(128)}, u32[]{:S(2)}) copy-start(s32[4]{0:T(128)} %param.24) | copy-start | bytes 52
  6.5 7.2 %copy-start.1 = (bf16[1,256,4096]{2,1,0:T(8,128)(2,1)S(1)}, bf16[1,256,4096]{2,1,0:T(8,128)(2,1)}, u32[]{:S(2)}) copy-start(bf16[1,256,4096]{2,1,0:T(8,128)(2,1)} %param.19) | copy-start | bytes 6291460
  6.5 46.6 %all-gather.2.cloned.1.call-start = ((), (), s32[]{:S(2)}) async-start(), calls=%async_computation.1 | async-start | bytes 2359296 | tf_op jit(solution)/shard_map/all_gather | solution.py:13
  14.3 1.8 copy-start.4
  14.3 2.6 %copy-start.2 = (bf16[1,256,4096]{2,1,0:T(8,128)(2,1)S(1)}, bf16[1,256,4096]{2,1,0:T(8,128)(2,1)}, u32[]{:S(2)}) copy-start(bf16[1,256,4096]{2,1,0:T(8,128)(2,1)} %param.20) | copy-start | bytes 6291460
  17.3 1.2 copy-start.3
  18.8 32.5 %copy-start.5 = (bf16[4,4,512]{2,1,0:T(4,128)(2,1)S(1)}, bf16[4,4,512]{2,1,0:T(4,128)(2,1)}, u32[]{:S(2)}) copy-start(bf16[4,4,512]{2,1,0:T(4,128)(2,1)} %param.25) | copy-start | bytes 49156
  18.8 32.5 %copy-start.6 = (bf16[512]{0:T(512)(128)(2,1)S(1)}, bf16[512]{0:T(512)(128)(2,1)}, u32[]{:S(2)}) copy-start(bf16[512]{0:T(512)(128)(2,1)} %param.27) | copy-start | bytes 3076
  20.6 124.4 %all-reduce.3.cloned.1.call-start = ((), (), s32[]{:S(2)}) async-start(), calls=%async_computation.2 | async-start | bytes 2097152 | tf_op jit(solution)/shard_map/psum | solution.py:152
  88.9 84.7 %reduce-scatter.2.cloned.1.call-start = ((), (), s32[]{:S(2)}) async-start(), calls=%async_computation.3 | async-start | bytes 163840 | tf_op jit(solution)/shard_map/reduce_scatter | solution.py:154
Sparse Core Ops, SparseCore 0:
  20.8 32.3 all-gather.1
  89.0 56.0 all-reduce.2
  150.7 22.7 reduce-scatter.1
where the time goes:
time: 182 us; the launch traced here: 181 us
  waiting for transfers between devices  80.9 us (44%)
  blocking collectives  53.5 us (29%)
  matrix products  16.5 us (9%)
  between operations  14.8 us (8%)
  local copies, waits for them, and re-layouts  11 us (6%)
  other arithmetic  4.55 us (2%)
    psum x1, waiting for transfers between devices, body(): summed = lax.psum(lifted, ('seq', 'mlp'))  56.1 us
    all_gather x2, blocking collectives, merged(): pieces = jax.tree.map(lambda part: lax.all_gather(part, axis), value)  29.9 us
    reduce_scatter x1, waiting for transfers between devices, body(): lax.psum_scatter(jnp.dot(activated, w_down, preferred_element_type=jnp.fl...  22.9 us
    psum x1, blocking collectives, body(): lax.psum((jnp.sum(stream, axis=1), jnp.sum(stream * stream, axis=1)), ('s...  15.5 us
    all_gather x1, blocking collectives, body(): lax.all_gather(hidden, 'grp', axis=0, tiled=True)  8.13 us
    dot_general x1, matrix products, body(): jnp.dot(activated, w_down, preferred_element_type=jnp.float32)  5.52 us
    dot_general x1, matrix products, body(): jnp.dot(lax.all_gather(hidden, 'grp', axis=0, tiled=True), w_up, preferre...  4.1 us
  transfers between devices with their start and end apart: 3, of which 3 were waited for; matrix products, arithmetic and copies ran while one was open for 0% of the time, Pallas kernels for 0%

commit v1 on v0

--- a/solution.py
+++ b/solution.py
@@ -7,6 +7,28 @@
 D = 4096
 H = 32
 NEG = -1e30
+
+
+def in_order(tiles, dim):
+    tiles = jnp.moveaxis(tiles, 0, dim)
+    shape = tiles.shape
+    return tiles.reshape(*shape[:dim], shape[dim] * shape[dim + 1], *shape[dim + 2 :])
+
+
+def gather_around(shard, axis, dim):
+    size = lax.axis_size(axis)
+    pairs = [(i, (i + 1) % size) for i in range(size)]
+    back = [(b, a) for a, b in pairs]
+    lower, upper = ([], [])
+    for hop in range(size - 1):
+        if hop % 2 == 0:
+            lower.append(lax.ppermute(lower[-1] if lower else shard, axis, pairs))
+        else:
+            upper.append(lax.ppermute(upper[-1] if upper else shard, axis, back))
+    tiles = jnp.stack([*lower[::-1], shard, *upper])
+    shift = lax.axis_index(axis) - len(lower)
+    tiles = tiles[(jnp.arange(size) - shift) % size]
+    return in_order(tiles, dim)
 
 
 def merged(value, axis, join):
@@ -146,9 +168,7 @@
         * lax.rsqrt(row_var[:, None] + 1e-05)
         * ln_gain.astype(jnp.float32)
     ).astype(jnp.bfloat16)
-    lifted = jnp.dot(
-        lax.all_gather(hidden, "grp", axis=0, tiled=True), w_up, preferred_element_type=jnp.float32
-    )
+    lifted = jnp.dot(gather_around(hidden, "grp", 0), w_up, preferred_element_type=jnp.float32)
     summed = lax.psum(lifted, ("seq", "mlp"))
     activated = jax.nn.gelu(summed, approximate=False).astype(jnp.bfloat16)
     projected = lax.psum_scatter(

time: 182 us -> 184 us (1.011)
  blocking collectives: 53.5 us -> 45.4 us
  waiting for transfers between devices: 80.9 us -> 86.6 us
  starting transfers between devices: 0.09 us -> 3.52 us
    all_gather x1 -> x0, blocking collectives: 8.13 us -> none  [body(): lax.all_gather(hidden, 'grp', axis=0, tiled=True)]
    ppermute x0 -> x3, waiting for transfers between devices: none -> 5.76 us  [the longest x2 5.74 us: gather_around(): lower.append(lax.ppermute(lower[-1] if lower else shard, axis, pairs))]
    ppermute x0 -> x3, starting transfers between devices: none -> 3.44 us  [the longest x2 1.92 us: gather_around(): lower.append(lax.ppermute(lower[-1] if lower else shard, axis, pairs))]
  transfers between devices with their start and end apart: 3 -> 6, of which waited for: 3 -> 5; matrix products, arithmetic and copies ran while one was open for 0% -> 0% of each run, Pallas kernels for 0% -> 0%
where the time goes in v1:
time: 184 us; the launch traced here: 183 us
  waiting for transfers between devices  86.6 us (47%)
  blocking collectives  45.4 us (25%)
  matrix products  16.4 us (9%)
  between operations  14.8 us (8%)
  local copies, waits for them, and re-layouts  11.6 us (6%)
  other arithmetic  4.66 us (3%)
  starting transfers between devices  3.52 us (2%)
    psum x1, waiting for transfers between devices, body(): summed = lax.psum(lifted, ('seq', 'mlp'))  56.1 us
    all_gather x2, blocking collectives, merged(): pieces = jax.tree.map(lambda part: lax.all_gather(part, axis), value)  29.9 us
    reduce_scatter x1, waiting for transfers between devices, body(): lax.psum_scatter(jnp.dot(activated, w_down, preferred_element_type=jnp.fl...  22.9 us
    psum x1, blocking collectives, body(): lax.psum((jnp.sum(stream, axis=1), jnp.sum(stream * stream, axis=1)), ('s...  15.5 us
    ppermute x2, waiting for transfers between devices, gather_around(): lower.append(lax.ppermute(lower[-1] if lower else shard, axis, pairs))  5.74 us
    dot_general x1, matrix products, body(): jnp.dot(activated, w_down, preferred_element_type=jnp.float32)  5.52 us
    dot_general x1, matrix products, body(): jnp.dot(gather_around(hidden, 'grp', 0), w_up, preferred_element_type=jnp...  4.07 us
  transfers between devices with their start and end apart: 6, of which 5 were waited for; matrix products, arithmetic and copies ran while one was open for 0% of the time, Pallas kernels for 0%

profile of v1, /device:TPU:0, one launch (start us, length us, event | category | flops | bytes accessed | tf_op | source)
XLA Modules:
  0.0 183.1 jit_solution(14550273696721715514)
XLA Ops:
  7.4 1.2 dynamic_slice.28
  9.9 1.1 reshape.234
  11.0 1.4 copy.98
  12.5 0.7 fusion.145
  14.4 1.2 fusion.144
  17.4 1.0 fusion.3
  19.8 0.8 copy.92
  21.0 15.8 %all_gather.29 = f32[8,16,32]{2,1,0:T(8,128)S(1)} all-gather(f32[1,16,32]{2,1,0:T(8,128)S(1)} %copy.83), channel_id=1, replica_groups=mesh['grp'=4,'seq'=4,'mlp'=2] {'seq','mlp'}, dimensions={0}, use_global_device_ids=true | all-gather | bytes 18432 | tf_op jit(solution)/shard_map/all_gather | solution.py:35
  37.2 14.1 %all_gather.26 = f32[8,16,32]{2,1,0:T(8,128)S(1)} all-gather(f32[1,16,32]{2,1,0:T(8,128)S(1)} %copy.76), channel_id=1, replica_groups=mesh['grp'=4,'seq'=4,'mlp'=2] {'seq','mlp'}, dimensions={0}, use_global_device_ids=true | all-gather | bytes 18432 | tf_op jit(solution)/shard_map/all_gather | solution.py:35
  51.4 1.7 all-gather.2.cloned.1.call-done
  53.1 1.7 slice.31
  54.8 1.0 slice_bitcast_fusion
  55.8 2.2 %while.14 = (s32[]{:T(128)}, f32[16,32]{1,0:T(8,128)S(1)}, f32[16,32]{1,0:T(8,128)S(1)}, f32[16,32,128]{2,1,0:T(8,128)S(1)}, f32[7,16,32]{2,1,0:T(8,128)S(1)}, /...) while((s32[]{:T(128)}, f32[16,32]{1,0:T(8,128)S(1)}, f32[16,32]{1,0:T(8,128)S(1)}, ...), condition=%wide.region_7.8_spmd, body=%wide.region_6.7_spmd.sunk | while | flops 199682 | bytes 807005 | solution.py:38
  58.1 3.0 %fusion.139 = (f32[16]{0:T(128)S(1)}, f32[16]{0:T(128)S(1)}, f32[16,512]{1,0:T(8,128)S(1)}) fusion(f32[16,512]{1,0:T(8,128)S(1)} %reshape.239, bf16[4096,512]{1,0:T(8,128)(2,1)} %param.26, bf16[2,8,32,128]{3,2,1,0:T(8,128)(2,1)S(1)} %bitcast.185), kind=kOutput, calls=%fused_computation.190 | convolution fusion | flops 67141600 | bytes 4391040 | tf_op jit(solution)/shard_map/dot_general | solution.py:158
  61.1 15.5 %all-reduce = (f32[16]{0:T(128)S(1)}, f32[16]{0:T(128)S(1)}) all-reduce(f32[16]{0:T(128)S(1)} %get-tuple-element.60, f32[16]{0:T(128)S(1)} %get-tuple-element.59), channel_id=1, replica_groups=mesh['grp'=4,'seq'=4,'mlp'=2] {'seq','mlp'}, use_global_device_ids=true, to_apply=%region_11.12 | all-reduce | flops 32 | bytes 256 | tf_op jit(solution)/shard_map/psum | solution.py:161
  76.6 1.4 collective-permute-start
  78.0 1.5 collective-permute-start.2
  79.6 1.7 collective-permute-done
  81.9 4.0 %collective-permute-done.1 = bf16[16,512]{1,0:T(8,128)(2,1)S(1)} collective-permute-done((bf16[16,512]{1,0:T(8,128)(2,1)S(1)}, bf16[16,512]{1,0:T(8,128)(2,1)S(1)}, u32[]{:S(2)}, u32[]{:S(2)}) %collective-permute-start.1) | collective-permute-done | bytes 16416 | tf_op jit(solution)/shard_map/ppermute | solution.py:25
  86.5 4.1 %fusion.146 = f32[64,4096]{1,0:T(8,128)} fusion(bf16[64,512]{1,0:T(8,128)(2,1)S(1)} %bitcast.187, bf16[512,4096]{1,0:T(8,128)(2,1)} %param.28), kind=kOutput, calls=%fused_computation.193 | convolution fusion | flops 268435456 | bytes 5308416 | tf_op jit(solution)/shard_map/dot_general | solution.py:171
  90.6 56.1 %all-reduce.3.cloned.1.call-done = f32[64,4096]{1,0:T(8,128)} async-done(((f32[64,4096]{1,0:T(8,128)}), f32[64,4096]{1,0:T(8,128)}) %all-reduce.3.cloned.1.call-update) | async-done | bytes 1048592 | tf_op jit(solution)/shard_map/psum | solution.py:172
  146.7 5.5 %fusion.37 = f32[64,512]{1,0:T(8,128)} fusion(bf16[4096,512]{1,0:T(8,128)(2,1)} %param.29, f32[64,4096]{1,0:T(8,128)} %all-reduce.3.cloned.1.call-done), kind=kOutput, calls=%fused_computation.50 | convolution fusion | flops 285474816 | bytes 5373952 | tf_op jit(solution)/shard_map/dot_general | solution.py:175
  152.3 22.9 %reduce-scatter.2.cloned.1.call-done = f32[16,512]{1,0:T(8,128)} async-done(((f32[64,512]{1,0:T(8,128)}), f32[16,512]{1,0:T(8,128)}) %reduce-scatter.2.cloned.1.call-update) | async-done | bytes 32784 | tf_op jit(solution)/shard_map/reduce_scatter | solution.py:174
  175.2 0.8 add.194
  (95 shorter events, 9.9 us)
Async XLA Ops:
  6.5 13.1 %copy-start = (bf16[1,4,4096]{2,1,0:T(4,128)(2,1)S(1)}, bf16[1,4,4096]{2,1,0:T(4,128)(2,1)}, u32[]{:S(2)}) copy-start(bf16[1,4,4096]{2,1,0:T(4,128)(2,1)} %param.18) | copy-start | bytes 98308
  6.5 7.1 %copy-start.7 = (s32[4]{0:T(128)S(1)}, s32[4]{0:T(128)}, u32[]{:S(2)}) copy-start(s32[4]{0:T(128)} %param.24) | copy-start | bytes 52
  6.5 7.2 %copy-start.1 = (bf16[1,256,4096]{2,1,0:T(8,128)(2,1)S(1)}, bf16[1,256,4096]{2,1,0:T(8,128)(2,1)}, u32[]{:S(2)}) copy-start(bf16[1,256,4096]{2,1,0:T(8,128)(2,1)} %param.19) | copy-start | bytes 6291460
  6.5 46.6 %all-gather.2.cloned.1.call-start = ((), (), s32[]{:S(2)}) async-start(), calls=%async_computation.1 | async-start | bytes 2359296 | tf_op jit(solution)/shard_map/all_gather | solution.py:35
  14.3 1.8 copy-start.4
  14.3 2.6 %copy-start.2 = (bf16[1,256,4096]{2,1,0:T(8,128)(2,1)S(1)}, bf16[1,256,4096]{2,1,0:T(8,128)(2,1)}, u32[]{:S(2)}) copy-start(bf16[1,256,4096]{2,1,0:T(8,128)(2,1)} %param.20) | copy-start | bytes 6291460
  17.4 1.2 copy-start.3
  18.8 32.5 %copy-start.5 = (bf16[4,4,512]{2,1,0:T(4,128)(2,1)S(1)}, bf16[4,4,512]{2,1,0:T(4,128)(2,1)}, u32[]{:S(2)}) copy-start(bf16[4,4,512]{2,1,0:T(4,128)(2,1)} %param.25) | copy-start | bytes 49156
  18.8 32.5 %copy-start.6 = (bf16[512]{0:T(512)(128)(2,1)S(1)}, bf16[512]{0:T(512)(128)(2,1)}, u32[]{:S(2)}) copy-start(bf16[512]{0:T(512)(128)(2,1)} %param.27) | copy-start | bytes 3076
  20.6 126.1 %all-reduce.3.cloned.1.call-start = ((), (), s32[]{:S(2)}) async-start(), calls=%async_computation.2 | async-start | bytes 2097152 | tf_op jit(solution)/shard_map/psum | solution.py:172
  76.6 4.6 %collective-permute-start = (bf16[16,512]{1,0:T(8,128)(2,1)S(1)}, bf16[16,512]{1,0:T(8,128)(2,1)S(1)}, u32[]{:S(2)}, u32[]{:S(2)}) collective-permute-start(bf16[16,512]{1,0:T(8,128)(2,1)S(1)} %multiply_convert_fusion), channel_id=1, source_target_pairs={{0,8},{8,16},{16,24},{24,0},{1,9},{9,17},{17,25},{25,1},{2,10},{10... | collective-permute-start | bytes 49160 | tf_op jit(solution)/shard_map/ppermute | solution.py:25
  78.0 3.8 %collective-permute-start.2 = (bf16[16,512]{1,0:T(8,128)(2,1)S(1)}, bf16[16,512]{1,0:T(8,128)(2,1)S(1)}, u32[]{:S(2)}, u32[]{:S(2)}) collective-permute-start(bf16[16,512]{1,0:T(8,128)(2,1)S(1)} %multiply_convert_fusion), channel_id=1, source_target_pairs={{8,0},{16,8},{24,16},{0,24},{9,1},{17,9},{25,17},{1,25},{10,2},{18... | collective-permute-start | bytes 49160 | tf_op jit(solution)/shard_map/ppermute | solution.py:27
  81.3 4.6 %collective-permute-start.1 = (bf16[16,512]{1,0:T(8,128)(2,1)S(1)}, bf16[16,512]{1,0:T(8,128)(2,1)S(1)}, u32[]{:S(2)}, u32[]{:S(2)}) collective-permute-start(bf16[16,512]{1,0:T(8,128)(2,1)S(1)} %collective-permute-done), channel_id=1, source_target_pairs={{0,8},{8,16},{16,24},{24,0},{1,9},{9,17},{17,25},{25,1},{2,10},{10... | collective-permute-start | bytes 49160 | tf_op jit(solution)/shard_map/ppermute | solution.py:25
  90.6 84.6 %reduce-scatter.2.cloned.1.call-start = ((), (), s32[]{:S(2)}) async-start(), calls=%async_computation.3 | async-start | bytes 163840 | tf_op jit(solution)/shard_map/reduce_scatter | solution.py:174
Sparse Core Ops, SparseCore 0:
  20.8 32.3 all-gather.1
  90.7 55.9 all-reduce.2
  152.4 22.7 reduce-scatter.1
